TPU v7x, 256 devices: a whole 4x4x8 slice. The times are simulated.
256 devices in a mesh: grp: 32 (over z_hi, x, core), sp: 8 (over y, z_lo).
Axes of the slice: x: 4, y: 4, z: 8 (z_hi: 4, z_lo: 2; z = z_hi * 2 + z_lo), core: 2. Of those that a mesh axis runs over, the one named last changes fastest.
Arguments:
- queries: bfloat16 [32, 2048, 4096], P('grp', 'sp'), may hold values from -22 to 22
- keys: bfloat16 [32, 2048, 1024], P('grp', 'sp'), may hold values from -16 to 16
- values: bfloat16 [32, 2048, 1024], P('grp', 'sp'), may hold values from -6 to 6
- page_owner: int32 [32, 128, 1], P('grp'), may hold values from 0 to 31; in each aligned block of 128 rows (0 to 127, 128 to 255, ..., all dimensions but the last counted through in order) at most 8 rows name the same one
Outputs:
- attention: bfloat16 [32, 2048, 4096], P('grp', 'sp')
- key_cache: bfloat16 [8192, 16, 1024], P('grp', None, 'sp')
- value_cache: bfloat16 [8192, 16, 1024], P('grp', None, 'sp')
Inputs may be any that keep to these rules, and one draw needn't show every extreme that they name: `page_owner`: for each prompt, no decode instance stores more than 8 of its pages, and in every draw some instance stores exactly 8 pages of some prompt.
All inputs are finite; a program needn't handle non-finite values.
Results may differ from a plain program's by a relative error of at most 0.0047.
Values may be sent and summed in bfloat16 or wider, within the bound.
No kernel may reach another device: no remote copies, remote signals or barrier semaphores. Data moves between devices by JAX's collectives and lax.ppermute only.
A program may use at most 128 MiB of HBM per device.

v0:
```python
import jax
import jax.numpy as jnp
from jax import lax
from jax.sharding import PartitionSpec as P

Q_HEADS = 32
KV_HEADS = 8
HEAD_DIM = 128
PAGE = 16
MOST = 8


def attend(queries, keys, values, first_pos, group):
    q_rows = queries.shape[0]
    k_rows = keys.shape[0]
    kv_local = keys.shape[1] // HEAD_DIM
    allowed = jnp.arange(k_rows)[None, None, :] <= first_pos + jnp.arange(q_rows)[None, :, None]
    scale = HEAD_DIM ** (-0.5)
    span = group * HEAD_DIM
    outputs = []
    for head in range(kv_local):
        query_block = queries[:, head * span : (head + 1) * span].reshape(q_rows, group, HEAD_DIM)
        key_head = keys[:, head * HEAD_DIM : (head + 1) * HEAD_DIM]
        value_head = values[:, head * HEAD_DIM : (head + 1) * HEAD_DIM]
        scores = (
            jnp.einsum("qgd,kd->gqk", query_block, key_head, preferred_element_type=jnp.float32)
            * scale
        )
        scores = jnp.where(allowed, scores, -jnp.inf)
        shifted = jnp.exp(scores - jnp.max(scores, axis=2, keepdims=True))
        weights = (shifted / jnp.sum(shifted, axis=2, keepdims=True)).astype(jnp.bfloat16)
        result = jnp.einsum(
            "gqk,kd->qgd", weights, value_head, preferred_element_type=jnp.float32
        ).astype(jnp.bfloat16)
        outputs.append(result.reshape(q_rows, span))
    return jnp.concatenate(outputs, axis=1)


def ship_pages(key_part, value_part, owners, count):
    width = key_part.shape[1]
    pages_n = key_part.shape[0] // PAGE
    stacked = jnp.concatenate(
        [key_part.reshape(pages_n, PAGE * width), value_part.reshape(pages_n, PAGE * width)], axis=1
    )
    onehot = (owners[:, None] == jnp.arange(count)[None, :]).astype(jnp.int32)
    rank = jnp.sum(onehot * (jnp.cumsum(onehot, axis=0) - 1), axis=1)
    target = owners * MOST + rank
    select = (jnp.arange(count * MOST)[:, None] == target[None, :]).astype(jnp.bfloat16)
    outgoing = jnp.dot(select, stacked, preferred_element_type=jnp.float32).astype(jnp.bfloat16)
    arrived = lax.all_to_all(outgoing, "grp", split_axis=0, concat_axis=0, tiled=True)
    key_cache = arrived[:, : PAGE * width].reshape(count * MOST, PAGE, width)
    value_cache = arrived[:, PAGE * width :].reshape(count * MOST, PAGE, width)
    return (key_cache, value_cache)


def local(queries, keys, values, page_owner):
    count = lax.axis_size("grp")
    ranks = lax.axis_size("sp")
    group = Q_HEADS // KV_HEADS
    all_keys, all_values = (
        lax.all_gather(keys, "sp", axis=1, tiled=True),
        lax.all_gather(values, "sp", axis=1, tiled=True),
    )
    local_rows = queries.shape[1]
    position = lax.axis_index("sp")
    output = attend(queries[0], all_keys[0], all_values[0], position * local_rows, group)
    attention = output[None]
    span = KV_HEADS * HEAD_DIM // ranks
    key_part = lax.dynamic_slice_in_dim(all_keys[0], position * span, span, 1)
    value_part = lax.dynamic_slice_in_dim(all_values[0], position * span, span, 1)
    key_cache, value_cache = ship_pages(key_part, value_part, page_owner[0, :, 0], count)
    return (attention, key_cache, value_cache)


def solution(mesh):
    placed = (
        P("grp", "sp", None),
        P("grp", "sp", None),
        P("grp", "sp", None),
        P("grp", None, None),
    )
    return jax.shard_map(
        local,
        mesh=mesh,
        in_specs=placed,
        out_specs=(P("grp", "sp", None), P("grp", None, "sp"), P("grp", None, "sp")),
        check_vma=False,
    )
```

profile of v0, /device:TPU:33, one launch (start us, length us, event | category | flops | bytes accessed | tf_op | source)
XLA Modules:
  0.0 338.2 jit_solution(8983498427392546353)
XLA Ops:
  7.2 0.7 all-gather.3.cloned.1.call-update
  7.9 2.0 copy.26
  10.0 3.3 copy.24
  13.3 0.7 fusion.85
  14.0 0.2 reduce_window_sum.11
  14.2 0.8 select_reduce_fusion
  15.1 0.7 multiply_add_fusion
  15.7 0.9 fusion.103
  16.6 0.3 iota_compare_fusion
  17.0 87.6 %all-gather.3.cloned.1.call-done = bf16[1,2048,1024]{2,1,0:T(8,128)(2,1)} async-done(((bf16[1,256,1024]{2,1,0:T(8,128)(2,1)}), bf16[1,2048,1024]{2,1,0:T(8,128)(2,1)}) %all-gather.3.cloned.1.call-update) | async-done | bytes 4194320 | tf_op jit(solution)/shard_map/all_gather | solution.py:61
  104.6 7.0 %fusion.105 = (f32[4,256]{1,0:T(4,128)S(1)}, f32[4,256,2048]{1,2,0:T(8,128)}) fusion(pred[256,2048]{0,1:T(8,128)(4,1)S(1)} %iota_compare_fusion, bf16[256,4,128]{0,2,1:T(8,128)(2,1)} %bitcast.282, bf16[2048,1024]{1,0:T(8,128)(2,1)} %bitcast.291), kind=kOutput, calls=%fused_computation.156 | convolution fusion | flops 545261568 | bytes 9703424 | tf_op jit(solution)/shard_map/sub | solution.py:30
  111.7 88.3 %all-gather.5.cloned.1.call-done = bf16[1,2048,1024]{1,2,0:T(8,128)(2,1)} async-done(((bf16[1,256,1024]{1,2,0:T(8,128)(2,1)}), bf16[1,2048,1024]{1,2,0:T(8,128)(2,1)}) %all-gather.5.cloned.1.call-update) | async-done | bytes 4194320 | tf_op jit(solution)/shard_map/all_gather | solution.py:62
  199.9 4.3 %fusion.55 = bf16[4,256,128]{1,2,0:T(8,128)(2,1)S(1)} fusion(f32[4,256,2048]{1,2,0:T(8,128)} %get-tuple-element.16, f32[4,256]{1,0:T(4,128)S(1)} %get-tuple-element.15, bf16[2048,1024]{0,1:T(8,128)(2,1)} %bitcast.299), kind=kOutput, calls=%fused_computation.81 | convolution fusion | flops 541196288 | bytes 9179136 | tf_op jit(solution)/shard_map/gqk,kd->qgd/dot_general | solution.py:32
  204.4 7.0 %fusion.104 = (f32[4,256]{1,0:T(4,128)S(1)}, f32[4,256,2048]{1,2,0:T(8,128)}) fusion(pred[256,2048]{0,1:T(8,128)(4,1)S(1)} %iota_compare_fusion, bf16[256,4,128]{0,2,1:T(8,128)(2,1)S(1)} %bitcast.281, bf16[2048,1024]{1,0:T(8,128)(2,1)} %bitcast.292), kind=kOutput, calls=%fused_computation.155 | convolution fusion | flops 545261568 | bytes 9703424 | tf_op jit(solution)/shard_map/sub | solution.py:30
  211.3 4.3 %fusion.56 = bf16[4,256,128]{1,2,0:T(8,128)(2,1)S(1)} fusion(f32[4,256,2048]{1,2,0:T(8,128)} %get-tuple-element.14, f32[4,256]{1,0:T(4,128)S(1)} %get-tuple-element.13, bf16[2048,1024]{0,1:T(8,128)(2,1)} %bitcast.300), kind=kOutput, calls=%fused_computation.82 | convolution fusion | flops 541196288 | bytes 9179136 | tf_op jit(solution)/shard_map/gqk,kd->qgd/dot_general | solution.py:32
  215.8 7.0 %fusion.106 = (f32[4,256]{1,0:T(4,128)S(1)}, f32[4,256,2048]{1,2,0:T(8,128)}) fusion(pred[256,2048]{0,1:T(8,128)(4,1)S(1)} %iota_compare_fusion, bf16[256,4,128]{0,2,1:T(8,128)(2,1)S(1)} %bitcast.280, bf16[2048,1024]{1,0:T(8,128)(2,1)} %bitcast.293), kind=kOutput, calls=%fused_computation.157 | convolution fusion | flops 545261568 | bytes 9703424 | tf_op jit(solution)/shard_map/sub | solution.py:30
  222.7 4.3 %fusion.54 = bf16[4,256,128]{1,2,0:T(8,128)(2,1)S(1)} fusion(f32[4,256,2048]{1,2,0:T(8,128)} %get-tuple-element.18, f32[4,256]{1,0:T(4,128)S(1)} %get-tuple-element.17, bf16[2048,1024]{0,1:T(8,128)(2,1)} %bitcast.301), kind=kOutput, calls=%fused_computation.80 | convolution fusion | flops 541196288 | bytes 9179136 | tf_op jit(solution)/shard_map/gqk,kd->qgd/dot_general | solution.py:32
  227.2 7.2 %fusion.107 = (f32[4,256]{1,0:T(4,128)S(1)}, f32[4,256,2048]{1,2,0:T(8,128)}) fusion(pred[256,2048]{0,1:T(8,128)(4,1)S(1)} %iota_compare_fusion, bf16[256,4,128]{0,2,1:T(8,128)(2,1)S(1)} %bitcast.279, bf16[2048,1024]{1,0:T(8,128)(2,1)} %bitcast.294), kind=kOutput, calls=%fused_computation.158 | convolution fusion | flops 545261568 | bytes 9703424 | tf_op jit(solution)/shard_map/sub | solution.py:30
  234.3 4.3 %fusion.53 = bf16[4,256,128]{1,2,0:T(8,128)(2,1)S(1)} fusion(f32[4,256,2048]{1,2,0:T(8,128)} %get-tuple-element.20, f32[4,256]{1,0:T(4,128)S(1)} %get-tuple-element.19, bf16[2048,1024]{0,1:T(8,128)(2,1)} %bitcast.302), kind=kOutput, calls=%fused_computation.79 | convolution fusion | flops 541196288 | bytes 9179136 | tf_op jit(solution)/shard_map/gqk,kd->qgd/dot_general | solution.py:32
  238.7 7.0 %fusion.108 = (f32[4,256]{1,0:T(4,128)S(1)}, f32[4,256,2048]{1,2,0:T(8,128)}) fusion(pred[256,2048]{0,1:T(8,128)(4,1)S(1)} %iota_compare_fusion, bf16[256,4,128]{0,2,1:T(8,128)(2,1)S(1)} %bitcast.278, bf16[2048,1024]{1,0:T(8,128)(2,1)} %bitcast.295), kind=kOutput, calls=%fused_computation.159 | convolution fusion | flops 545261568 | bytes 9703424 | tf_op jit(solution)/shard_map/sub | solution.py:30
  245.7 4.3 %fusion.52 = bf16[4,256,128]{1,2,0:T(8,128)(2,1)S(1)} fusion(f32[4,256,2048]{1,2,0:T(8,128)} %get-tuple-element.22, f32[4,256]{1,0:T(4,128)S(1)} %get-tuple-element.21, bf16[2048,1024]{0,1:T(8,128)(2,1)} %bitcast.303), kind=kOutput, calls=%fused_computation.78 | convolution fusion | flops 541196288 | bytes 9179136 | tf_op jit(solution)/shard_map/gqk,kd->qgd/dot_general | solution.py:32
  250.2 7.0 %fusion.109 = (f32[4,256]{1,0:T(4,128)S(1)}, f32[4,256,2048]{1,2,0:T(8,128)}) fusion(pred[256,2048]{0,1:T(8,128)(4,1)S(1)} %iota_compare_fusion, bf16[256,4,128]{0,2,1:T(8,128)(2,1)S(1)} %bitcast.277, bf16[2048,1024]{1,0:T(8,128)(2,1)} %bitcast.296), kind=kOutput, calls=%fused_computation.160 | convolution fusion | flops 545261568 | bytes 9703424 | tf_op jit(solution)/shard_map/sub | solution.py:30
  257.1 4.3 %fusion.51 = bf16[4,256,128]{1,2,0:T(8,128)(2,1)S(1)} fusion(f32[4,256,2048]{1,2,0:T(8,128)} %get-tuple-element.24, f32[4,256]{1,0:T(4,128)S(1)} %get-tuple-element.23, bf16[2048,1024]{0,1:T(8,128)(2,1)} %bitcast.304), kind=kOutput, calls=%fused_computation.77 | convolution fusion | flops 541196288 | bytes 9179136 | tf_op jit(solution)/shard_map/gqk,kd->qgd/dot_general | solution.py:32
  261.4 0.8 copy.47
  262.3 1.1 constant_dynamic-slice_fusion.1
  263.3 0.3 copy.50
  263.6 0.2 reshape.142
  263.8 1.1 constant_dynamic-slice_fusion
  264.9 0.2 reshape.141
  265.2 2.0 fusion.16
  267.2 10.3 %all-to-all-start = ((bf16[32,8,4096]{2,1,0:T(8,128)(2,1)}), bf16[32,8,4096]{2,1,0:T(8,128)(2,1)S(1)}, u32[]{:S(2)}, u32[]{:S(2)}) async-start(bf16[32,8,4096]{2,1,0:T(8,128)(2,1)} %fusion.16), calls=%async_computation | async-start | bytes 4194304 | tf_op jit(solution)/shard_map/all_to_all | solution.py:50
  277.5 7.2 %fusion.110 = (f32[4,256]{1,0:T(4,128)S(1)}, f32[4,256,2048]{1,2,0:T(8,128)}) fusion(pred[256,2048]{0,1:T(8,128)(4,1)} %copy-done, bf16[256,4,128]{0,2,1:T(8,128)(2,1)} %bitcast.276, bf16[2048,1024]{1,0:T(8,128)(2,1)} %bitcast.297), kind=kOutput, calls=%fused_computation.161 | convolution fusion | flops 545261568 | bytes 9703424 | tf_op jit(solution)/shard_map/sub | solution.py:30
  284.7 5.0 %fusion.50 = bf16[4,256,128]{1,2,0:T(8,128)(2,1)} fusion(f32[4,256,2048]{1,2,0:T(8,128)} %get-tuple-element.26, f32[4,256]{1,0:T(4,128)S(1)} %get-tuple-element.25, bf16[2048,1024]{0,1:T(8,128)(2,1)} %bitcast.305), kind=kOutput, calls=%fused_computation.76 | convolution fusion | flops 541196288 | bytes 9179136 | tf_op jit(solution)/shard_map/gqk,kd->qgd/dot_general | solution.py:32
  289.7 1.8 copy.48
  291.5 7.2 %fusion.111 = (f32[4,256]{1,0:T(4,128)S(1)}, f32[4,256,2048]{1,2,0:T(8,128)}) fusion(pred[256,2048]{0,1:T(8,128)(4,1)} %copy-done, bf16[256,4,128]{0,2,1:T(8,128)(2,1)} %bitcast.275, bf16[2048,1024]{1,0:T(8,128)(2,1)} %bitcast.298), kind=kOutput, calls=%fused_computation.162 | convolution fusion | flops 545261568 | bytes 9703424 | tf_op jit(solution)/shard_map/sub | solution.py:30
  298.7 5.0 %fusion.49 = bf16[4,256,128]{1,2,0:T(8,128)(2,1)} fusion(f32[4,256,2048]{1,2,0:T(8,128)} %get-tuple-element.28, f32[4,256]{1,0:T(4,128)S(1)} %get-tuple-element.27, bf16[2048,1024]{0,1:T(8,128)(2,1)} %bitcast.306), kind=kOutput, calls=%fused_computation.75 | convolution fusion | flops 541196288 | bytes 9179136 | tf_op jit(solution)/shard_map/gqk,kd->qgd/dot_general | solution.py:32
  303.7 1.8 copy.49
  305.5 0.7 constant_dynamic-update-slice_fusion.7
  306.2 0.7 constant_dynamic-update-slice_fusion.6
  307.0 0.7 constant_dynamic-update-slice_fusion.5
  307.7 0.7 constant_dynamic-update-slice_fusion.4
  308.4 0.7 constant_dynamic-update-slice_fusion.3
  309.1 1.7 constant_dynamic-update-slice_fusion.2
  310.8 1.7 constant_dynamic-update-slice_fusion.1
  312.5 1.7 constant_dynamic-update-slice_fusion
  314.1 14.7 %all-to-all-done = bf16[32,8,4096]{2,1,0:T(8,128)(2,1)S(1)} async-done(((bf16[32,8,4096]{2,1,0:T(8,128)(2,1)}), bf16[32,8,4096]{2,1,0:T(8,128)(2,1)S(1)}, u32[]{:S(2)}, u32[]{:S(2)}) %all-to-all-start) | async-done | bytes 2097184 | tf_op jit(solution)/shard_map/all_to_all | solution.py:50
  329.0 1.2 copy.67
  330.2 1.2 copy.68
  (12 shorter events, 0.9 us)
Async XLA Ops:
  7.2 97.4 %all-gather.3.cloned.1.call-start = ((), (), s32[]{:S(2)}) async-start(), calls=%async_computation.1 | async-start | bytes 4718592 | tf_op jit(solution)/shard_map/all_gather | solution.py:61
  7.9 192.0 %all-gather.5.cloned.1.call-start = ((), (), s32[]{:S(2)}) async-start(), calls=%async_computation.2 | async-start | bytes 4718592 | tf_op jit(solution)/shard_map/all_gather | solution.py:62
  17.0 233.2 %copy-start = (pred[256,2048]{0,1:T(8,128)(4,1)}, pred[256,2048]{0,1:T(8,128)(4,1)S(1)}, u32[]{:S(2)}) copy-start(pred[256,2048]{0,1:T(8,128)(4,1)S(1)} %iota_compare_fusion) | copy-start | bytes 1572868
  267.2 61.6 %all-to-all-start = ((bf16[32,8,4096]{2,1,0:T(8,128)(2,1)}), bf16[32,8,4096]{2,1,0:T(8,128)(2,1)S(1)}, u32[]{:S(2)}, u32[]{:S(2)}) async-start(bf16[32,8,4096]{2,1,0:T(8,128)(2,1)} %fusion.16), calls=%async_computation | async-start | bytes 4194304 | tf_op jit(solution)/shard_map/all_to_all | solution.py:50
Sparse Core Ops, SparseCore 0:
  9.8 94.7 all-gather.2
  106.9 92.9 all-gather.4
where the time goes:
time: 339 us; the launch traced here: 338 us
  waiting for transfers between devices  191 us (56%)
  matrix products  94.2 us (28%)
  local copies, waits for them, and re-layouts  25.4 us (7%)
  between operations  14.2 us (4%)
  starting transfers between devices  10.3 us (3%)
    all_gather x1, waiting for transfers between devices, local(): lax.all_gather(values, 'sp', axis=1, tiled=True)  88.3 us
    all_gather x1, waiting for transfers between devices, local(): lax.all_gather(keys, 'sp', axis=1, tiled=True)  87.6 us
    sub x8, matrix products, attend(): shifted = jnp.exp(scores - jnp.max(scores, axis=2, keepdims=True))  56.5 us
    dot_general x8, matrix products, attend(): jnp.einsum('gqk,kd->qgd', weights, value_head, preferred_element_type=jnp...  35.7 us
    unnamed x14, local copies, waits for them, and re-layouts  14.8 us
    all_to_all x1, waiting for transfers between devices, ship_pages(): lax.all_to_all(outgoing, 'grp', split_axis=0, concat_axis=0, tiled=True)  14.7 us
    all_to_all x1, starting transfers between devices, ship_pages(): lax.all_to_all(outgoing, 'grp', split_axis=0, concat_axis=0, tiled=True)  10.3 us
  transfers between devices with their start and end apart: 3, of which 3 were waited for; matrix products, arithmetic and copies ran while one was open for 16% of the time, Pallas kernels for 0%

commit v1 on v0

v1 whole, which is shorter than its diff:
```python
import functools

import jax
import jax.numpy as jnp
from jax import lax
from jax.experimental import pallas as pl
from jax.experimental.pallas import tpu as pltpu
from jax.sharding import Mesh, PartitionSpec as P

Q_HEADS = 32
KV_HEADS = 8
HEAD_DIM = 128
GROUP = Q_HEADS // KV_HEADS
SPAN = GROUP * HEAD_DIM
PAIR = 2 * HEAD_DIM
PAGE = 16
MOST = 8
LOG2E = 1.4426950408889634
SCALE2 = HEAD_DIM**-0.5 * LOG2E
GRP = ("zh", "x", "core")
SP = ("y", "zl")
YS = 4
ZS = 2


def call(kernel, outs, ins, copies=1, scratch=(), space=pltpu.VMEM, out_space=None, vmem=12, name=None, flops=0, moved=0, exps=0):
    out_space = out_space or space
    return pl.pallas_call(
        kernel,
        out_shape=outs,
        in_specs=[pl.BlockSpec(memory_space=pltpu.SMEM if x.dtype == jnp.int32 else space) for x in ins],
        out_specs=jax.tree.map(lambda _: pl.BlockSpec(memory_space=out_space), outs),
        scratch_shapes=[*scratch, *([pltpu.SemaphoreType.DMA((copies,))] if out_space == pl.ANY else [])],
        compiler_params=pltpu.CompilerParams(vmem_limit_bytes=vmem * 2**20),
        cost_estimate=pl.CostEstimate(flops=flops, bytes_accessed=moved, transcendentals=exps),
        name=name,
    )(*ins)


def move(pairs, sem, first=0):
    copies = [pltpu.make_async_copy(src, dst, sem.at[first + i]) for i, (src, dst) in enumerate(pairs)]
    for copy in copies:
        copy.start()
    for copy in copies:
        copy.wait()


def columns(ref, start, width):
    return ref.at[:, pl.ds(pl.multiple_of(start, width), width)]


def pair_of(k_ref, v_ref, head):
    return jnp.concatenate([columns(r, head * HEAD_DIM, HEAD_DIM)[...] for r in (k_ref, v_ref)], axis=1)


def kv_send_kernel(k_ref, v_ref, o_ref, k, v, out, sem):
    move([(k_ref, k), (v_ref, v)], sem)
    for h in range(KV_HEADS):
        out[h] = pair_of(k, v, h)
    move([(out, o_ref)], sem, 2)


def q_send_kernel(where_ref, q_ref, k_ref, v_ref, *o_refs):
    y, z = where_ref[0], where_ref[1]
    for d in range(YS):
        head = lax.rem(y + d, YS) * ZS + z
        o_refs[d][...] = columns(q_ref, head * SPAN, SPAN)[...]
    for d in range(YS):
        head = lax.rem(y + d, YS) * ZS + 1 - z
        o_refs[YS + d][:, :SPAN] = columns(q_ref, head * SPAN, SPAN)[...]
        o_refs[YS + d][:, SPAN:] = pair_of(k_ref, v_ref, head)


def swap_send_kernel(where_ref, kv_ref, o_ref):
    for j in range(YS):
        o_ref[j] = kv_ref[2 * j + where_ref[1]]


def gather_out_kernel(where_ref, *refs):
    y, z = where_ref[0], where_ref[1]
    for c in range(ZS):
        for d in range(YS):
            head = lax.rem(y + YS - d, YS) * ZS + jnp.bitwise_xor(z, c)
            columns(refs[-1], head * SPAN, SPAN)[...] = refs[c * YS + d][...]


def slots_kernel(target_ref, kv_ref, o_ref, slots, sem):
    pages = kv_ref.shape[1] // PAGE
    copies = []
    for t in (0, 1):
        part = slice(t * PAGE, (t + 1) * PAGE)
        slots[:, part, :] = jnp.zeros((slots.shape[0], PAGE, HEAD_DIM), slots.dtype)
        for b in range(kv_ref.shape[0]):
            for p in range(pages):
                rows = kv_ref[b, p * PAGE : (p + 1) * PAGE, t * HEAD_DIM : (t + 1) * HEAD_DIM]
                slots[target_ref[b * pages + p], part, :] = rows
        copies.append(pltpu.make_async_copy(slots.at[:, part, :], o_ref.at[:, part, :], sem.at[t]))
        copies[t].start()
    for copy in copies:
        copy.wait()


def caches_kernel(a_ref, k_ref, v_ref, parts, sem):
    count = parts.shape[0]
    slots = parts.shape[1]
    here = [pl.ds(i * slots, slots) for i in range(count)]
    into = [pltpu.make_async_copy(a_ref.at[here[i]], parts.at[i], sem.at[i]) for i in range(count)]
    for copy in into:
        copy.start()
    out = []
    for i in range(count):
        into[i].wait()
        for t, o_ref in enumerate((k_ref, v_ref)):
            part = parts.at[i, :, t * PAGE : (t + 1) * PAGE, :]
            out.append(pltpu.make_async_copy(part, o_ref.at[here[i]], sem.at[count + 2 * i + t]))
            out[-1].start()
    for copy in out:
        copy.wait()


def attend_kernel(rows, stored, where_ref, *refs):
    in_refs, o_refs, (q_all, kv_all, o_all, sem) = refs[: -YS - 4], refs[-YS - 4 : -4], refs[-4:]
    y, z = where_ref[0], where_ref[1]
    pairs = []
    for d in range(YS):
        j = lax.rem(y + YS - d, YS)
        part, more = in_refs[d], in_refs[YS]
        if stored:
            pairs += [(part, q_all.at[j])]
            pairs += [(more.at[2 * d + z], kv_all.at[0, d]), (more.at[2 * d + 1 - z], kv_all.at[1, d])]
        else:
            pairs += [(part.at[:, :SPAN], q_all.at[j]), (part.at[:, SPAN:], kv_all.at[0, j]), (more.at[d], kv_all.at[1, d])]
    move(pairs, sem)
    later = z == 1
    keep = lax.broadcasted_iota(jnp.int32, (rows, rows), 1) <= lax.broadcasted_iota(jnp.int32, (rows, rows), 0)
    dims = (((1,), (1,)), ((), ()))
    ones = jnp.ones((rows, HEAD_DIM), jnp.bfloat16)
    for i in range(YS):
        for h in range(GROUP):
            q = q_all[i, :, h * HEAD_DIM : (h + 1) * HEAD_DIM]
            parts = []
            for j in range(i + 1):
                for far in (0, 1):
                    s = lax.dot_general(q, kv_all[far, j, :, :HEAD_DIM], dims, preferred_element_type=jnp.float32)
                    if j == i:
                        s = jnp.where(later if far else keep, s, -jnp.inf)
                    parts.append((j, far, s))
            top = functools.reduce(jnp.maximum, [s for _, _, s in parts])
            top = jnp.max(top, axis=1, keepdims=True) * SCALE2
            total = jnp.zeros((rows, PAIR), jnp.float32)
            for j, far, s in parts:
                p = jnp.exp2(s * SCALE2 - top).astype(jnp.bfloat16)
                v = jnp.concatenate([kv_all[far, j, :, HEAD_DIM:], ones], axis=1)
                total += jnp.dot(p, v, preferred_element_type=jnp.float32)
            out = total[:, :HEAD_DIM] / total[:, HEAD_DIM:]
            o_all[i, :, h * HEAD_DIM : (h + 1) * HEAD_DIM] = out.astype(jnp.bfloat16)
    move([(o_all.at[lax.rem(y + d, YS)], o_refs[d]) for d in range(YS)], sem, len(pairs))


def across_z(x):
    return lax.ppermute(x, "zl", [(0, 1), (1, 0)])


def along_y(parts):
    got = [parts[0]] + [None] * (YS - 1)
    for d in (2, 1, 3):
        got[d] = lax.ppermute(parts[d], "y", [(i, (i + d) % YS) for i in range(YS)])
    return got


def local(queries, keys, values, page_owner):
    count = lax.axis_size(GRP)
    rows = queries.shape[1]
    bf16 = lambda *shape: jax.ShapeDtypeStruct(shape, jnp.bfloat16)
    where = jnp.stack([lax.axis_index("y"), lax.axis_index("zl")]).astype(jnp.int32)

    k, v, q = keys[0], values[0], queries[0]
    kv_send = call(
        kv_send_kernel,
        bf16(KV_HEADS, rows, PAIR),
        (k, v),
        3,
        scratch=[
            pltpu.VMEM(k.shape, jnp.bfloat16),
            pltpu.VMEM(v.shape, jnp.bfloat16),
            pltpu.VMEM((KV_HEADS, rows, PAIR), jnp.bfloat16),
        ],
        space=pl.ANY,
        vmem=60,
        name="kv_send",
        moved=2 * 2**20,
    )
    owners = page_owner[0, :, 0]
    onehot = (owners[:, None] == jnp.arange(count)[None, :]).astype(jnp.int32)
    rank = jnp.sum(onehot * (jnp.cumsum(onehot, axis=0) - 1), axis=1)
    target = owners * MOST + rank
    kv_send, q, k, v = lax.optimization_barrier((kv_send, q, k, v))
    kv = lax.all_to_all(kv_send, SP, split_axis=0, concat_axis=0, tiled=True)
    *q_parts, r0, r1, r2, r3 = call(
        q_send_kernel,
        [bf16(rows, SPAN)] * YS + [bf16(rows, SPAN + PAIR)] * YS,
        (where, q, k, v),
        name="q_send",
        moved=5 * 2**20,
    )
    rest = [r0, r1, r2, r3]
    q_got = along_y(q_parts)
    swapped = across_z(
        call(swap_send_kernel, bf16(YS, rows, PAIR), (where, kv), name="swap_send", moved=2**20)
    )

    slots = call(
        slots_kernel,
        bf16(count * MOST, 2 * PAGE, HEAD_DIM),
        (target, kv),
        2,
        scratch=[pltpu.VMEM((count * MOST, 2 * PAGE, HEAD_DIM), jnp.bfloat16)],
        out_space=pl.ANY,
        name="slots",
        moved=3 * 2**20,
    )
    slots, rest = lax.optimization_barrier((slots, rest))
    kv, swapped = lax.optimization_barrier((kv, swapped))
    arrived = lax.all_to_all(slots, GRP, split_axis=0, concat_axis=0, tiled=True)
    key_cache, value_cache = call(
        caches_kernel,
        [bf16(count * MOST, PAGE, HEAD_DIM)] * 2,
        (arrived,),
        12,
        scratch=[pltpu.VMEM((4, count * MOST // 4, 2 * PAGE, HEAD_DIM), jnp.bfloat16)],
        space=pl.ANY,
        name="caches",
        moved=4 * 2**20,
    )

    rest_got = along_y(rest)
    got = []
    for stored, ins in ((True, (*q_got, kv)), (False, (*rest_got, swapped))):
        o_parts = call(
            functools.partial(attend_kernel, rows, stored),
            [bf16(rows, SPAN)] * YS,
            (where, *ins),
            4 * YS,
            scratch=[
                pltpu.VMEM((YS, rows, SPAN), jnp.bfloat16),
                pltpu.VMEM((ZS, YS, rows, PAIR), jnp.bfloat16),
                pltpu.VMEM((YS, rows, SPAN), jnp.bfloat16),
            ],
            space=pl.ANY,
            vmem=20,
            name="attend",
            flops=(200 if stored else 10) * 10**9,
            moved=4 * 2**20,
            exps=5 * 10**6,
        )
        got += along_y(o_parts)
    attention = call(
        gather_out_kernel,
        bf16(rows, Q_HEADS * HEAD_DIM),
        (where, *got),
        name="gather_out",
        moved=4 * 2**20,
    )
    return attention[None], key_cache, value_cache


def solution(mesh):
    parts = Mesh(mesh.devices.reshape(4, 4, 2, YS, ZS), GRP + SP)
    return jax.shard_map(
        local,
        mesh=parts,
        in_specs=(P(GRP, SP, None), P(GRP, SP, None), P(GRP, SP, None), P(GRP, None, None)),
        out_specs=(P(GRP, SP, None), P(GRP, None, SP), P(GRP, None, SP)),
        check_vma=False,
    )
```

time: 339 us -> 95.9 us (0.28)
  waiting for transfers between devices: 191 us -> 22.3 us
  matrix products: 94.2 us -> 0 us
  Pallas kernels: 0 us -> 31.7 us
  starting transfers between devices: 10.3 us -> 36.9 us
  local copies, waits for them, and re-layouts: 25.4 us -> 2.8 us
  between operations: 14.2 us -> 0.94 us
    all_gather x2 -> x0, waiting for transfers between devices: 176 us -> none  [the longest x1 88.3 us: local(): lax.all_gather(values, 'sp', axis=1, tiled=True)]
    sub x8 -> x0, matrix products: 56.5 us -> none  [attend(): shifted = jnp.exp(scores - jnp.max(scores, axis=2, keepdims=True))]
    dot_general x9 -> x0, matrix products: 37.8 us -> none  [the longest x8 35.7 us: attend(): jnp.einsum('gqk,kd->qgd', weights, value_head, preferred_element_type=jnp...]
    pallas_call x0 -> x8, Pallas kernels: none -> 31.7 us  [call(): pl.pallas_call(kernel, out_shape=outs, in_specs=[pl.BlockSpec(memory_spac...]
    ppermute x0 -> x13, starting transfers between devices: none -> 18.5 us  [the longest x12 17.4 us: along_y(): got[d] = lax.ppermute(parts[d], 'y', [(i, (i + d) % YS) for i in range(YS)])]
    ppermute x0 -> x13, waiting for transfers between devices: none -> 15.1 us  [the longest x12 15.1 us: along_y(): got[d] = lax.ppermute(parts[d], 'y', [(i, (i + d) % YS) for i in range(YS)])]
    unnamed x14 -> x12, local copies, waits for them, and re-layouts: 14.8 us -> 2.8 us
    all_to_all x1 -> x2, starting transfers between devices: 10.3 us -> 18.5 us  [the longest x1 13.1 us: local(): lax.all_to_all(slots, GRP, split_axis=0, concat_axis=0, tiled=True)]
  transfers between devices with their start and end apart: 3 -> 15, of which waited for: 3 -> 5; matrix products, arithmetic and copies ran while one was open for 16% -> 1% of each run, Pallas kernels for 0% -> 28%
where the time goes in v1:
time: 95.9 us; the launch traced here: 95.2 us
  starting transfers between devices  36.9 us (38%)
  Pallas kernels  31.7 us (33%)
  waiting for transfers between devices  22.3 us (23%)
  local copies, waits for them, and re-layouts  2.8 us (3%)
    pallas_call x8, Pallas kernels, call(): pl.pallas_call(kernel, out_shape=outs, in_specs=[pl.BlockSpec(memory_spac...  31.7 us
    ppermute x12, starting transfers between devices, along_y(): got[d] = lax.ppermute(parts[d], 'y', [(i, (i + d) % YS) for i in range(YS)])  17.4 us
    ppermute x12, waiting for transfers between devices, along_y(): got[d] = lax.ppermute(parts[d], 'y', [(i, (i + d) % YS) for i in range(YS)])  15.1 us
    all_to_all x1, starting transfers between devices, local(): lax.all_to_all(slots, GRP, split_axis=0, concat_axis=0, tiled=True)  13.1 us
    all_to_all x1, starting transfers between devices, local(): kv = lax.all_to_all(kv_send, SP, split_axis=0, concat_axis=0, tiled=True)  5.38 us
    all_to_all x1, waiting for transfers between devices, local(): kv = lax.all_to_all(kv_send, SP, split_axis=0, concat_axis=0, tiled=True)  4.11 us
    all_to_all x1, waiting for transfers between devices, local(): lax.all_to_all(slots, GRP, split_axis=0, concat_axis=0, tiled=True)  3.06 us
    unnamed x12, local copies, waits for them, and re-layouts  2.8 us
  transfers between devices with their start and end apart: 15, of which 5 were waited for; matrix products, arithmetic and copies ran while one was open for 1% of the time, Pallas kernels for 28%

profile of v1, /device:TPU:33, one launch (start us, length us, event | category | flops | bytes accessed | tf_op | source)
XLA Modules:
  0.0 95.2 jit_solution(11327413059692311860)
XLA Ops:
  0.6 0.0 copy-start
  0.6 2.5 %kv_send.1 = bf16[8,256,256]{2,1,0:T(8,128)(2,1)} custom-call(bf16[256,1024]{1,0:T(8,128)(2,1)} %bitcast.9, bf16[256,1024]{1,0:T(8,128)(2,1)} %bitcast.11), custom_call_target="tpu_custom_call" | custom-call | bytes 2097152 | tf_op jit(solution)/shard_map/kv_send/pallas_call | solution.py:28
  3.1 5.4 %all-to-all-start = ((bf16[8,256,256]{2,1,0:T(8,128)(2,1)}), bf16[8,256,256]{2,1,0:T(8,128)(2,1)S(1)}, u32[]{:S(2)}, u32[]{:S(2)}) async-start(bf16[8,256,256]{2,1,0:T(8,128)(2,1)} %kv_send.1), calls=%async_computation | async-start | bytes 2097152 | tf_op jit(solution)/shard_map/all_to_all | solution.py:198
  8.5 0.1 pad_add_fusion.where_ref
  8.6 0.0 copy-done
  8.6 1.0 %copy-done.1 = bf16[1,256,1024]{2,1,0:T(8,128)(2,1)S(1)} copy-done((bf16[1,256,1024]{2,1,0:T(8,128)(2,1)S(1)}, bf16[1,256,1024]{2,1,0:T(8,128)(2,1)}, u32[]{:S(2)}) %copy-start.1) | copy-done | bytes 524312
  9.6 1.0 %copy-done.2 = bf16[1,256,1024]{2,1,0:T(8,128)(2,1)S(1)} copy-done((bf16[1,256,1024]{2,1,0:T(8,128)(2,1)S(1)}, bf16[1,256,1024]{2,1,0:T(8,128)(2,1)}, u32[]{:S(2)}) %copy-start.2) | copy-done | bytes 524312
  10.7 2.0 %q_send.1 = (bf16[256,512]{1,0:T(8,128)(2,1)S(1)}, bf16[256,512]{1,0:T(8,128)(2,1)}, bf16[256,512]{1,0:T(8,128)(2,1)}, bf16[256,512]{1,0:T(8,128)(2,1)}, bf16[25...) custom-call(s32[2]{0:T(128)S(1)} %pad_add_fusion.where_ref, ...), custom_call_target="tpu_custom_call" | custom-call | bytes 5242880 | tf_op jit(solution)/shard_map/q_send/pallas_call | solution.py:28
  12.7 0.7 copy-done.3
  13.4 1.2 %collective-permute-start = (bf16[256,512]{1,0:T(8,128)(2,1)}, bf16[256,512]{1,0:T(8,128)(2,1)S(1)}, u32[]{:S(2)}, u32[]{:S(2)}) collective-permute-start(bf16[256,512]{1,0:T(8,128)(2,1)} %get-tuple-element.36), channel_id=1, source_target_pairs={{0,2},{2,4},{4,6},{6,0},{1,3},{3,5},{5,7},{7,1},{8,10},{10,12},{12... | collective-permute-start | bytes 786440 | tf_op jit(solution)/shard_map/ppermute | solution.py:167
  14.6 2.4 %collective-permute-start.1 = (bf16[256,512]{1,0:T(8,128)(2,1)}, bf16[256,512]{1,0:T(8,128)(2,1)S(1)}, u32[]{:S(2)}, u32[]{:S(2)}) collective-permute-start(bf16[256,512]{1,0:T(8,128)(2,1)} %get-tuple-element.37), channel_id=1, source_target_pairs={{0,4},{2,6},{4,0},{6,2},{1,5},{3,7},{5,1},{7,3},{8,12},{10,14},{12... | collective-permute-start | bytes 786440 | tf_op jit(solution)/shard_map/ppermute | solution.py:167
  17.0 1.2 %collective-permute-start.2 = (bf16[256,512]{1,0:T(8,128)(2,1)}, bf16[256,512]{1,0:T(8,128)(2,1)S(1)}, u32[]{:S(2)}, u32[]{:S(2)}) collective-permute-start(bf16[256,512]{1,0:T(8,128)(2,1)} %get-tuple-element.38), channel_id=1, source_target_pairs={{0,6},{2,0},{4,2},{6,4},{1,7},{3,1},{5,3},{7,5},{8,14},{10,8},{12,... | collective-permute-start | bytes 786440 | tf_op jit(solution)/shard_map/ppermute | solution.py:167
  18.2 4.1 %all-to-all-done.kv_ref.refs_4_ = bf16[8,256,256]{2,1,0:T(8,128)(2,1)S(1)} async-done(((bf16[8,256,256]{2,1,0:T(8,128)(2,1)}), bf16[8,256,256]{2,1,0:T(8,128)(2,1)S(1)}, u32[]{:S(2)}, u32[]{:S(2)}) %all-to-all-start) | async-done | bytes 1048608 | tf_op jit(solution)/shard_map/all_to_all | solution.py:198
  22.3 0.6 swap_send.1
  22.9 1.1 %collective-permute-start.3 = (bf16[4,256,256]{2,1,0:T(8,128)(2,1)S(1)}, bf16[4,256,256]{2,1,0:T(8,128)(2,1)S(1)}, u32[]{:S(2)}, u32[]{:S(2)}) collective-permute-start(bf16[4,256,256]{2,1,0:T(8,128)(2,1)S(1)} %swap_send.1), channel_id=1, source_target_pairs={{0,1},{1,0},{2,3},{3,2},{4,5},{5,4},{6,7},{7,6},{8,9},{9,8},{10,11... | collective-permute-start | bytes 1572872 | tf_op jit(solution)/shard_map/ppermute | solution.py:161
  24.0 0.0 copy-done.5
  24.0 0.1 fusion
  24.1 0.2 reduce_window_sum.11
  24.2 0.2 select_reduce_fusion
  24.4 2.1 %slots.1 = bf16[256,32,128]{2,1,0:T(8,128)(2,1)} custom-call(s32[128]{0:T(128)S(1)} %multiply_add_fusion.target_ref, bf16[8,256,256]{2,1,0:T(8,128)(2,1)S(1)} %all-to-all-done.kv_ref.refs_4_), custom_call_target="tpu_custom_call" | custom-call | bytes 3145728 | tf_op jit(solution)/shard_map/slots/pallas_call | solution.py:28
  26.6 0.9 collective-permute-start.7
  27.4 13.1 %all-to-all-start.1 = ((bf16[256,32,128]{2,1,0:T(8,128)(2,1)}), bf16[256,32,128]{2,1,0:T(8,128)(2,1)}, u32[]{:S(2)}, u32[]{:S(2)}) async-start(bf16[256,32,128]{2,1,0:T(8,128)(2,1)} %slots.1), calls=%async_computation.1 | async-start | bytes 4194304 | tf_op jit(solution)/shard_map/all_to_all | solution.py:224
  40.5 0.0 collective-permute-done.3.refs_4_
  40.5 1.9 %collective-permute-start.8 = (bf16[256,768]{1,0:T(8,128)(2,1)}, bf16[256,768]{1,0:T(8,128)(2,1)}, u32[]{:S(2)}, u32[]{:S(2)}) collective-permute-start(bf16[256,768]{1,0:T(8,128)(2,1)} %get-tuple-element.51), channel_id=1, source_target_pairs={{0,4},{2,6},{4,0},{6,2},{1,5},{3,7},{5,1},{7,3},{8,12},{10,14},{12... | collective-permute-start | bytes 1179656 | tf_op jit(solution)/shard_map/ppermute | solution.py:167
  42.4 0.0 collective-permute-done.refs_1_
  42.4 0.8 collective-permute-start.9
  43.3 0.0 collective-permute-done.1.refs_2_
  43.3 0.0 collective-permute-done.2.refs_3_
  43.3 9.9 %attend.2 = (bf16[256,512]{1,0:T(8,128)(2,1)S(1)}, bf16[256,512]{1,0:T(8,128)(2,1)S(1)}, bf16[256,512]{1,0:T(8,128)(2,1)S(1)}, bf16[256,512]{1,0:T(8,128)(2,1)S(1)}) custom-call(s32[2]{0:T(128)S(1)} %pad_add_fusion.where_ref, bf16[256,512]{1,0:T(8,128)(2,1)S(1)} %copy-done.4, bf16[256,512]{1,0:T(8,128)(2,1)S(1)} %collective-permute-done.refs_1_, ...), custom_call_target="tpu_custom_call" | custom-call | flops 199999995904 | bytes 4194304 | tf_op jit(solution)/shard_map/attend/pallas_call | solution.py:28
  53.2 0.7 collective-permute-start.4
  53.9 1.6 %collective-permute-start.5 = (bf16[256,512]{1,0:T(8,128)(2,1)S(1)}, bf16[256,512]{1,0:T(8,128)(2,1)S(1)}, u32[]{:S(2)}, u32[]{:S(2)}) collective-permute-start(bf16[256,512]{1,0:T(8,128)(2,1)S(1)} %get-tuple-element.43), channel_id=1, source_target_pairs={{0,4},{2,6},{4,0},{6,2},{1,5},{3,7},{5,1},{7,3},{8,12},{10,14},{12... | collective-permute-start | bytes 786440 | tf_op jit(solution)/shard_map/ppermute | solution.py:167
  55.5 0.0 collective-permute-done.7.refs_1_
  55.5 2.0 %collective-permute-start.6 = (bf16[256,512]{1,0:T(8,128)(2,1)S(1)}, bf16[256,512]{1,0:T(8,128)(2,1)S(1)}, u32[]{:S(2)}, u32[]{:S(2)}) collective-permute-start(bf16[256,512]{1,0:T(8,128)(2,1)S(1)} %get-tuple-element.44), channel_id=1, source_target_pairs={{0,6},{2,0},{4,2},{6,4},{1,7},{3,1},{5,3},{7,5},{8,14},{10,8},{12,... | collective-permute-start | bytes 786440 | tf_op jit(solution)/shard_map/ppermute | solution.py:167
  57.4 0.0 collective-permute-done.8.refs_2_
  57.5 3.8 %collective-permute-done.9.refs_3_ = bf16[256,768]{1,0:T(8,128)(2,1)} collective-permute-done((bf16[256,768]{1,0:T(8,128)(2,1)}, bf16[256,768]{1,0:T(8,128)(2,1)}, u32[]{:S(2)}, u32[]{:S(2)}) %collective-permute-start.9) | collective-permute-done | bytes 393248 | tf_op jit(solution)/shard_map/ppermute | solution.py:167
  61.3 10.1 %attend.3 = (bf16[256,512]{1,0:T(8,128)(2,1)S(1)}, bf16[256,512]{1,0:T(8,128)(2,1)S(1)}, bf16[256,512]{1,0:T(8,128)(2,1)S(1)}, bf16[256,512]{1,0:T(8,128)(2,1)S(1)}) custom-call(s32[2]{0:T(128)S(1)} %pad_add_fusion.where_ref, bf16[256,768]{1,0:T(8,128)(2,1)S(1)} %get-tuple-element.49.refs_0_, bf16[256,768]{1,0:T(8,128)(2,1)} %collective-permute-done.7.refs_1_, ...), custom_call_target="tpu_custom_call" | custom-call | flops 10000000000 | bytes 4194304 | tf_op jit(solution)/shard_map/attend/pallas_call | solution.py:28
  71.3 1.0 %collective-permute-start.10 = (bf16[256,512]{1,0:T(8,128)(2,1)S(1)}, bf16[256,512]{1,0:T(8,128)(2,1)S(1)}, u32[]{:S(2)}, u32[]{:S(2)}) collective-permute-start(bf16[256,512]{1,0:T(8,128)(2,1)S(1)} %get-tuple-element.55), channel_id=1, source_target_pairs={{0,2},{2,4},{4,6},{6,0},{1,3},{3,5},{5,7},{7,1},{8,10},{10,12},{12... | collective-permute-start | bytes 786440 | tf_op jit(solution)/shard_map/ppermute | solution.py:167
  72.4 3.8 %collective-permute-start.11 = (bf16[256,512]{1,0:T(8,128)(2,1)S(1)}, bf16[256,512]{1,0:T(8,128)(2,1)S(1)}, u32[]{:S(2)}, u32[]{:S(2)}) collective-permute-start(bf16[256,512]{1,0:T(8,128)(2,1)S(1)} %get-tuple-element.56), channel_id=1, source_target_pairs={{0,4},{2,6},{4,0},{6,2},{1,5},{3,7},{5,1},{7,3},{8,12},{10,14},{12... | collective-permute-start | bytes 786440 | tf_op jit(solution)/shard_map/ppermute | solution.py:167
  76.1 0.0 collective-permute-done.4.refs_1_
  76.1 0.0 collective-permute-start.12
  76.2 0.0 collective-permute-done.5.refs_2_
  76.2 0.0 collective-permute-done.6.refs_3_
  76.2 4.2 %collective-permute-done.10.refs_5_ = bf16[256,512]{1,0:T(8,128)(2,1)S(1)} collective-permute-done((bf16[256,512]{1,0:T(8,128)(2,1)S(1)}, bf16[256,512]{1,0:T(8,128)(2,1)S(1)}, u32[]{:S(2)}, u32[]{:S(2)}) %collective-permute-start.10) | collective-permute-done | bytes 262176 | tf_op jit(solution)/shard_map/ppermute | solution.py:167
  80.4 7.0 %collective-permute-done.11.refs_6_ = bf16[256,512]{1,0:T(8,128)(2,1)S(1)} collective-permute-done((bf16[256,512]{1,0:T(8,128)(2,1)S(1)}, bf16[256,512]{1,0:T(8,128)(2,1)S(1)}, u32[]{:S(2)}, u32[]{:S(2)}) %collective-permute-start.11) | collective-permute-done | bytes 262176 | tf_op jit(solution)/shard_map/ppermute | solution.py:167
  87.4 0.0 collective-permute-done.12.refs_7_
  87.4 2.0 %gather_out.1 = bf16[256,4096]{1,0:T(8,128)(2,1)} custom-call(s32[2]{0:T(128)S(1)} %pad_add_fusion.where_ref, bf16[256,512]{1,0:T(8,128)(2,1)S(1)} %get-tuple-element.41.refs_0_, bf16[256,512]{1,0:T(8,128)(2,1)S(1)} %collective-permute-done.4.refs_1_, bf16[256,512]{1,0:T(8,128)(2,1)S(1)} %collective-permute-done.5.refs_2_, ...), custom_call_target="tpu_custom_call" | custom-call | bytes 4194304 | tf_op jit(solution)/shard_map/gather_out/pallas_call | solution.py:28
  89.5 3.1 %all-to-all-done.1.a_ref = bf16[256,32,128]{2,1,0:T(8,128)(2,1)} async-done(((bf16[256,32,128]{2,1,0:T(8,128)(2,1)}), bf16[256,32,128]{2,1,0:T(8,128)(2,1)}, u32[]{:S(2)}, u32[]{:S(2)}) %all-to-all-start.1) | async-done | bytes 2097184 | tf_op jit(solution)/shard_map/all_to_all | solution.py:224
  92.5 2.4 %caches.1 = (bf16[256,16,128]{2,1,0:T(8,128)(2,1)}, bf16[256,16,128]{2,1,0:T(8,128)(2,1)}) custom-call(bf16[256,32,128]{2,1,0:T(8,128)(2,1)} %all-to-all-done.1.a_ref), custom_call_target="tpu_custom_call" | custom-call | bytes 4194304 | tf_op jit(solution)/shard_map/caches/pallas_call | solution.py:28
  (7 shorter events, 0.0 us)
Async XLA Ops:
  0.6 8.0 %copy-start = (bf16[1,256,4096]{2,1,0:T(8,128)(2,1)S(1)}, bf16[1,256,4096]{2,1,0:T(8,128)(2,1)}, u32[]{:S(2)}) copy-start(bf16[1,256,4096]{2,1,0:T(8,128)(2,1)} %param.4) | copy-start | bytes 6291460
  3.1 19.2 %all-to-all-start = ((bf16[8,256,256]{2,1,0:T(8,128)(2,1)}), bf16[8,256,256]{2,1,0:T(8,128)(2,1)S(1)}, u32[]{:S(2)}, u32[]{:S(2)}) async-start(bf16[8,256,256]{2,1,0:T(8,128)(2,1)} %kv_send.1), calls=%async_computation | async-start | bytes 2097152 | tf_op jit(solution)/shard_map/all_to_all | solution.py:198
  8.6 1.0 %copy-start.1 = (bf16[1,256,1024]{2,1,0:T(8,128)(2,1)S(1)}, bf16[1,256,1024]{2,1,0:T(8,128)(2,1)}, u32[]{:S(2)}) copy-start(bf16[1,256,1024]{2,1,0:T(8,128)(2,1)} %param.5) | copy-start | bytes 1572868
  9.6 1.0 %copy-start.2 = (bf16[1,256,1024]{2,1,0:T(8,128)(2,1)S(1)}, bf16[1,256,1024]{2,1,0:T(8,128)(2,1)}, u32[]{:S(2)}) copy-start(bf16[1,256,1024]{2,1,0:T(8,128)(2,1)} %param.6) | copy-start | bytes 1572868
  10.7 13.3 %copy-start.5 = (s32[1,128,1]{1,2,0:T(1,128)S(1)}, s32[1,128,1]{1,2,0:T(1,128)}, u32[]{:S(2)}) copy-start(s32[1,128,1]{1,2,0:T(1,128)} %param.7) | copy-start | bytes 1540
  12.7 0.7 copy-start.3
  13.4 29.0 %collective-permute-start = (bf16[256,512]{1,0:T(8,128)(2,1)}, bf16[256,512]{1,0:T(8,128)(2,1)S(1)}, u32[]{:S(2)}, u32[]{:S(2)}) collective-permute-start(bf16[256,512]{1,0:T(8,128)(2,1)} %get-tuple-element.36), channel_id=1, source_target_pairs={{0,2},{2,4},{4,6},{6,0},{1,3},{3,5},{5,7},{7,1},{8,10},{10,12},{12... | collective-permute-start | bytes 786440 | tf_op jit(solution)/shard_map/ppermute | solution.py:167
  14.6 28.6 %collective-permute-start.1 = (bf16[256,512]{1,0:T(8,128)(2,1)}, bf16[256,512]{1,0:T(8,128)(2,1)S(1)}, u32[]{:S(2)}, u32[]{:S(2)}) collective-permute-start(bf16[256,512]{1,0:T(8,128)(2,1)} %get-tuple-element.37), channel_id=1, source_target_pairs={{0,4},{2,6},{4,0},{6,2},{1,5},{3,7},{5,1},{7,3},{8,12},{10,14},{12... | collective-permute-start | bytes 786440 | tf_op jit(solution)/shard_map/ppermute | solution.py:167
  17.0 26.2 %collective-permute-start.2 = (bf16[256,512]{1,0:T(8,128)(2,1)}, bf16[256,512]{1,0:T(8,128)(2,1)S(1)}, u32[]{:S(2)}, u32[]{:S(2)}) collective-permute-start(bf16[256,512]{1,0:T(8,128)(2,1)} %get-tuple-element.38), channel_id=1, source_target_pairs={{0,6},{2,0},{4,2},{6,4},{1,7},{3,1},{5,3},{7,5},{8,14},{10,8},{12,... | collective-permute-start | bytes 786440 | tf_op jit(solution)/shard_map/ppermute | solution.py:167
  22.9 17.6 %collective-permute-start.3 = (bf16[4,256,256]{2,1,0:T(8,128)(2,1)S(1)}, bf16[4,256,256]{2,1,0:T(8,128)(2,1)S(1)}, u32[]{:S(2)}, u32[]{:S(2)}) collective-permute-start(bf16[4,256,256]{2,1,0:T(8,128)(2,1)S(1)} %swap_send.1), channel_id=1, source_target_pairs={{0,1},{1,0},{2,3},{3,2},{4,5},{5,4},{6,7},{7,6},{8,9},{9,8},{10,11... | collective-permute-start | bytes 1572872 | tf_op jit(solution)/shard_map/ppermute | solution.py:161
  26.6 16.7 %copy-start.4 = (bf16[256,512]{1,0:T(8,128)(2,1)S(1)}, bf16[256,512]{1,0:T(8,128)(2,1)}, u32[]{:S(2)}) copy-start(bf16[256,512]{1,0:T(8,128)(2,1)} %copy-done.3) | copy-start | bytes 786436
  26.6 28.9 %collective-permute-start.7 = (bf16[256,768]{1,0:T(8,128)(2,1)}, bf16[256,768]{1,0:T(8,128)(2,1)}, u32[]{:S(2)}, u32[]{:S(2)}) collective-permute-start(bf16[256,768]{1,0:T(8,128)(2,1)} %get-tuple-element.50), channel_id=1, source_target_pairs={{0,2},{2,4},{4,6},{6,0},{1,3},{3,5},{5,7},{7,1},{8,10},{10,12},{12... | collective-permute-start | bytes 1179656 | tf_op jit(solution)/shard_map/ppermute | solution.py:167
  27.4 65.1 %all-to-all-start.1 = ((bf16[256,32,128]{2,1,0:T(8,128)(2,1)}), bf16[256,32,128]{2,1,0:T(8,128)(2,1)}, u32[]{:S(2)}, u32[]{:S(2)}) async-start(bf16[256,32,128]{2,1,0:T(8,128)(2,1)} %slots.1), calls=%async_computation.1 | async-start | bytes 4194304 | tf_op jit(solution)/shard_map/all_to_all | solution.py:224
  40.5 16.9 %collective-permute-start.8 = (bf16[256,768]{1,0:T(8,128)(2,1)}, bf16[256,768]{1,0:T(8,128)(2,1)}, u32[]{:S(2)}, u32[]{:S(2)}) collective-permute-start(bf16[256,768]{1,0:T(8,128)(2,1)} %get-tuple-element.51), channel_id=1, source_target_pairs={{0,4},{2,6},{4,0},{6,2},{1,5},{3,7},{5,1},{7,3},{8,12},{10,14},{12... | collective-permute-start | bytes 1179656 | tf_op jit(solution)/shard_map/ppermute | solution.py:167
  42.4 18.8 %collective-permute-start.9 = (bf16[256,768]{1,0:T(8,128)(2,1)}, bf16[256,768]{1,0:T(8,128)(2,1)}, u32[]{:S(2)}, u32[]{:S(2)}) collective-permute-start(bf16[256,768]{1,0:T(8,128)(2,1)} %get-tuple-element.52), channel_id=1, source_target_pairs={{0,6},{2,0},{4,2},{6,4},{1,7},{3,1},{5,3},{7,5},{8,14},{10,8},{12,... | collective-permute-start | bytes 1179656 | tf_op jit(solution)/shard_map/ppermute | solution.py:167
  53.2 22.9 %collective-permute-start.4 = (bf16[256,512]{1,0:T(8,128)(2,1)S(1)}, bf16[256,512]{1,0:T(8,128)(2,1)S(1)}, u32[]{:S(2)}, u32[]{:S(2)}) collective-permute-start(bf16[256,512]{1,0:T(8,128)(2,1)S(1)} %get-tuple-element.42), channel_id=1, source_target_pairs={{0,2},{2,4},{4,6},{6,0},{1,3},{3,5},{5,7},{7,1},{8,10},{10,12},{12... | collective-permute-start | bytes 786440 | tf_op jit(solution)/shard_map/ppermute | solution.py:167
  53.9 22.2 %collective-permute-start.5 = (bf16[256,512]{1,0:T(8,128)(2,1)S(1)}, bf16[256,512]{1,0:T(8,128)(2,1)S(1)}, u32[]{:S(2)}, u32[]{:S(2)}) collective-permute-start(bf16[256,512]{1,0:T(8,128)(2,1)S(1)} %get-tuple-element.43), channel_id=1, source_target_pairs={{0,4},{2,6},{4,0},{6,2},{1,5},{3,7},{5,1},{7,3},{8,12},{10,14},{12... | collective-permute-start | bytes 786440 | tf_op jit(solution)/shard_map/ppermute | solution.py:167
  55.5 20.7 %collective-permute-start.6 = (bf16[256,512]{1,0:T(8,128)(2,1)S(1)}, bf16[256,512]{1,0:T(8,128)(2,1)S(1)}, u32[]{:S(2)}, u32[]{:S(2)}) collective-permute-start(bf16[256,512]{1,0:T(8,128)(2,1)S(1)} %get-tuple-element.44), channel_id=1, source_target_pairs={{0,6},{2,0},{4,2},{6,4},{1,7},{3,1},{5,3},{7,5},{8,14},{10,8},{12,... | collective-permute-start | bytes 786440 | tf_op jit(solution)/shard_map/ppermute | solution.py:167
  71.3 9.1 %collective-permute-start.10 = (bf16[256,512]{1,0:T(8,128)(2,1)S(1)}, bf16[256,512]{1,0:T(8,128)(2,1)S(1)}, u32[]{:S(2)}, u32[]{:S(2)}) collective-permute-start(bf16[256,512]{1,0:T(8,128)(2,1)S(1)} %get-tuple-element.55), channel_id=1, source_target_pairs={{0,2},{2,4},{4,6},{6,0},{1,3},{3,5},{5,7},{7,1},{8,10},{10,12},{12... | collective-permute-start | bytes 786440 | tf_op jit(solution)/shard_map/ppermute | solution.py:167
  72.4 15.1 %collective-permute-start.11 = (bf16[256,512]{1,0:T(8,128)(2,1)S(1)}, bf16[256,512]{1,0:T(8,128)(2,1)S(1)}, u32[]{:S(2)}, u32[]{:S(2)}) collective-permute-start(bf16[256,512]{1,0:T(8,128)(2,1)S(1)} %get-tuple-element.56), channel_id=1, source_target_pairs={{0,4},{2,6},{4,0},{6,2},{1,5},{3,7},{5,1},{7,3},{8,12},{10,14},{12... | collective-permute-start | bytes 786440 | tf_op jit(solution)/shard_map/ppermute | solution.py:167
  76.1 11.3 %collective-permute-start.12 = (bf16[256,512]{1,0:T(8,128)(2,1)S(1)}, bf16[256,512]{1,0:T(8,128)(2,1)S(1)}, u32[]{:S(2)}, u32[]{:S(2)}) collective-permute-start(bf16[256,512]{1,0:T(8,128)(2,1)S(1)} %get-tuple-element.57), channel_id=1, source_target_pairs={{0,6},{2,0},{4,2},{6,4},{1,7},{3,1},{5,3},{7,5},{8,14},{10,8},{12,... | collective-permute-start | bytes 786440 | tf_op jit(solution)/shard_map/ppermute | solution.py:167

commit v2 on v1

--- a/solution.py
+++ b/solution.py
@@ -21,6 +21,8 @@
 SP = ("y", "zl")
 YS = 4
 ZS = 2
+FIRST = (0, 1, 2, 3)
+SHIFTS = (0, 2, 1, 3)
 
 
 def call(kernel, outs, ins, copies=1, scratch=(), space=pltpu.VMEM, out_space=None, vmem=12, name=None, flops=0, moved=0, exps=0):
@@ -54,21 +56,38 @@
 
 
 def kv_send_kernel(k_ref, v_ref, o_ref, k, v, out, sem):
-    move([(k_ref, k), (v_ref, v)], sem)
-    for h in range(KV_HEADS):
-        out[h] = pair_of(k, v, h)
-    move([(out, o_ref)], sem, 2)
+    rows = k.shape[0] // 2
+    halves = [slice(i * rows, (i + 1) * rows) for i in (0, 1)]
+    into = [
+        pltpu.make_async_copy(src.at[half], dst.at[half], sem.at[2 * i + t])
+        for i, half in enumerate(halves)
+        for t, (src, dst) in enumerate(((k_ref, k), (v_ref, v)))
+    ]
+    for copy in into:
+        copy.start()
+    away = []
+    for i, half in enumerate(halves):
+        into[2 * i].wait()
+        into[2 * i + 1].wait()
+        for h in range(KV_HEADS):
+            cols = slice(h * HEAD_DIM, (h + 1) * HEAD_DIM)
+            out[h, half, :HEAD_DIM] = k[half, cols]
+            out[h, half, HEAD_DIM:] = v[half, cols]
+        away.append(pltpu.make_async_copy(out.at[:, half], o_ref.at[:, half], sem.at[4 + i]))
+        away[i].start()
+    for copy in away:
+        copy.wait()
 
 
 def q_send_kernel(where_ref, q_ref, k_ref, v_ref, *o_refs):
     y, z = where_ref[0], where_ref[1]
-    for d in range(YS):
+    for n, d in enumerate(FIRST):
         head = lax.rem(y + d, YS) * ZS + z
-        o_refs[d][...] = columns(q_ref, head * SPAN, SPAN)[...]
-    for d in range(YS):
+        o_refs[n][...] = columns(q_ref, head * SPAN, SPAN)[...]
+    for n, d in enumerate(SHIFTS):
         head = lax.rem(y + d, YS) * ZS + 1 - z
-        o_refs[YS + d][:, :SPAN] = columns(q_ref, head * SPAN, SPAN)[...]
-        o_refs[YS + d][:, SPAN:] = pair_of(k_ref, v_ref, head)
+        o_refs[YS + n][:, :SPAN] = columns(q_ref, head * SPAN, SPAN)[...]
+        o_refs[YS + n][:, SPAN:] = pair_of(k_ref, v_ref, head)
 
 
 def swap_send_kernel(where_ref, kv_ref, o_ref):
@@ -79,9 +98,9 @@
 def gather_out_kernel(where_ref, *refs):
     y, z = where_ref[0], where_ref[1]
     for c in range(ZS):
-        for d in range(YS):
+        for n, d in enumerate(SHIFTS):
             head = lax.rem(y + YS - d, YS) * ZS + jnp.bitwise_xor(z, c)
-            columns(refs[-1], head * SPAN, SPAN)[...] = refs[c * YS + d][...]
+            columns(refs[-1], head * SPAN, SPAN)[...] = refs[c * YS + n][...]
 
 
 def slots_kernel(target_ref, kv_ref, o_ref, slots, sem):
@@ -122,14 +141,14 @@
     in_refs, o_refs, (q_all, kv_all, o_all, sem) = refs[: -YS - 4], refs[-YS - 4 : -4], refs[-4:]
     y, z = where_ref[0], where_ref[1]
     pairs = []
-    for d in range(YS):
+    for n, d in enumerate(FIRST if stored else SHIFTS):
         j = lax.rem(y + YS - d, YS)
-        part, more = in_refs[d], in_refs[YS]
+        part, more = in_refs[n], in_refs[YS]
         if stored:
             pairs += [(part, q_all.at[j])]
-            pairs += [(more.at[2 * d + z], kv_all.at[0, d]), (more.at[2 * d + 1 - z], kv_all.at[1, d])]
+            pairs += [(more.at[2 * n + z], kv_all.at[0, n]), (more.at[2 * n + 1 - z], kv_all.at[1, n])]
         else:
-            pairs += [(part.at[:, :SPAN], q_all.at[j]), (part.at[:, SPAN:], kv_all.at[0, j]), (more.at[d], kv_all.at[1, d])]
+            pairs += [(part.at[:, :SPAN], q_all.at[j]), (part.at[:, SPAN:], kv_all.at[0, j]), (more.at[n], kv_all.at[1, n])]
     move(pairs, sem)
     later = z == 1
     keep = lax.broadcasted_iota(jnp.int32, (rows, rows), 1) <= lax.broadcasted_iota(jnp.int32, (rows, rows), 0)
@@ -154,18 +173,18 @@
                 total += jnp.dot(p, v, preferred_element_type=jnp.float32)
             out = total[:, :HEAD_DIM] / total[:, HEAD_DIM:]
             o_all[i, :, h * HEAD_DIM : (h + 1) * HEAD_DIM] = out.astype(jnp.bfloat16)
-    move([(o_all.at[lax.rem(y + d, YS)], o_refs[d]) for d in range(YS)], sem, len(pairs))
+    move([(o_all.at[lax.rem(y + d, YS)], o_refs[n]) for n, d in enumerate(SHIFTS)], sem, len(pairs))
 
 
 def across_z(x):
     return lax.ppermute(x, "zl", [(0, 1), (1, 0)])
 
 
-def along_y(parts):
-    got = [parts[0]] + [None] * (YS - 1)
-    for d in (2, 1, 3):
-        got[d] = lax.ppermute(parts[d], "y", [(i, (i + d) % YS) for i in range(YS)])
-    return got
+def along_y(parts, shifts=SHIFTS):
+    return [
+        lax.ppermute(part, "y", [(i, (i + d) % YS) for i in range(YS)]) if d else part
+        for part, d in zip(parts, shifts, strict=True)
+    ]
 
 
 def local(queries, keys, values, page_owner):
@@ -179,7 +198,7 @@
         kv_send_kernel,
         bf16(KV_HEADS, rows, PAIR),
         (k, v),
-        3,
+        6,
         scratch=[
             pltpu.VMEM(k.shape, jnp.bfloat16),
             pltpu.VMEM(v.shape, jnp.bfloat16),
@@ -204,7 +223,7 @@
         moved=5 * 2**20,
     )
     rest = [r0, r1, r2, r3]
-    q_got = along_y(q_parts)
+    q_got = along_y(q_parts, FIRST)
     swapped = across_z(
         call(swap_send_kernel, bf16(YS, rows, PAIR), (where, kv), name="swap_send", moved=2**20)
     )
@@ -219,8 +238,7 @@
         name="slots",
         moved=3 * 2**20,
     )
-    slots, rest = lax.optimization_barrier((slots, rest))
-    kv, swapped = lax.optimization_barrier((kv, swapped))
+    kv, swapped, rest = lax.optimization_barrier((kv, swapped, rest))
     arrived = lax.all_to_all(slots, GRP, split_axis=0, concat_axis=0, tiled=True)
     key_cache, value_cache = call(
         caches_kernel,

time: 95.9 us -> 96.4 us (level)
  the two profiles are of different devices: /device:TPU:33 before, /device:TPU:1 now
where the time goes in v2:
time: 96.4 us; the launch traced here: 96 us
  starting transfers between devices  36.5 us (38%)
  Pallas kernels  31.5 us (33%)
  waiting for transfers between devices  23.7 us (25%)
  local copies, waits for them, and re-layouts  2.8 us (3%)
    pallas_call x8, Pallas kernels, call(): pl.pallas_call(kernel, out_shape=outs, in_specs=[pl.BlockSpec(memory_spac...  31.5 us
    ppermute x12, waiting for transfers between devices, along_y(): lax.ppermute(part, 'y', [(i, (i + d) % YS) for i in range(YS)])  17.1 us
    ppermute x12, starting transfers between devices, along_y(): lax.ppermute(part, 'y', [(i, (i + d) % YS) for i in range(YS)])  15.5 us
    all_to_all x1, starting transfers between devices, local(): lax.all_to_all(slots, GRP, split_axis=0, concat_axis=0, tiled=True)  14.1 us
    all_to_all x1, starting transfers between devices, local(): kv = lax.all_to_all(kv_send, SP, split_axis=0, concat_axis=0, tiled=True)  6.39 us
    all_to_all x1, waiting for transfers between devices, local(): kv = lax.all_to_all(kv_send, SP, split_axis=0, concat_axis=0, tiled=True)  4.81 us
    unnamed x12, local copies, waits for them, and re-layouts  2.8 us
  transfers between devices with their start and end apart: 15, of which 5 were waited for; matrix products, arithmetic and copies ran while one was open for 1% of the time, Pallas kernels for 28%

profile of v2, /device:TPU:1, one launch (start us, length us, event | category | flops | bytes accessed | tf_op | source)
XLA Modules:
  0.0 96.0 jit_solution(8169001437810485401)
XLA Ops:
  0.6 0.0 copy-start
  0.6 2.3 %kv_send.1 = bf16[8,256,256]{2,1,0:T(8,128)(2,1)} custom-call(bf16[256,1024]{1,0:T(8,128)(2,1)} %bitcast.9, bf16[256,1024]{1,0:T(8,128)(2,1)} %bitcast.11), custom_call_target="tpu_custom_call" | custom-call | bytes 2097152 | tf_op jit(solution)/shard_map/kv_send/pallas_call | solution.py:30
  2.9 6.4 %all-to-all-start = ((bf16[8,256,256]{2,1,0:T(8,128)(2,1)}), bf16[8,256,256]{2,1,0:T(8,128)(2,1)S(1)}, u32[]{:S(2)}, u32[]{:S(2)}) async-start(bf16[8,256,256]{2,1,0:T(8,128)(2,1)} %kv_send.1), calls=%async_computation | async-start | bytes 2097152 | tf_op jit(solution)/shard_map/all_to_all | solution.py:217
  9.3 0.1 pad_add_fusion.where_ref
  9.4 0.0 copy-done
  9.4 1.0 %copy-done.1 = bf16[1,256,1024]{2,1,0:T(8,128)(2,1)S(1)} copy-done((bf16[1,256,1024]{2,1,0:T(8,128)(2,1)S(1)}, bf16[1,256,1024]{2,1,0:T(8,128)(2,1)}, u32[]{:S(2)}) %copy-start.1) | copy-done | bytes 524312
  10.4 1.0 %copy-done.2 = bf16[1,256,1024]{2,1,0:T(8,128)(2,1)S(1)} copy-done((bf16[1,256,1024]{2,1,0:T(8,128)(2,1)S(1)}, bf16[1,256,1024]{2,1,0:T(8,128)(2,1)}, u32[]{:S(2)}) %copy-start.2) | copy-done | bytes 524312
  11.5 2.0 %q_send.1 = (bf16[256,512]{1,0:T(8,128)(2,1)S(1)}, bf16[256,512]{1,0:T(8,128)(2,1)}, bf16[256,512]{1,0:T(8,128)(2,1)}, bf16[256,512]{1,0:T(8,128)(2,1)}, bf16[25...) custom-call(s32[2]{0:T(128)S(1)} %pad_add_fusion.where_ref, ...), custom_call_target="tpu_custom_call" | custom-call | bytes 5242880 | tf_op jit(solution)/shard_map/q_send/pallas_call | solution.py:30
  13.5 0.7 copy-done.3
  14.2 1.5 %collective-permute-start = (bf16[256,512]{1,0:T(8,128)(2,1)}, bf16[256,512]{1,0:T(8,128)(2,1)S(1)}, u32[]{:S(2)}, u32[]{:S(2)}) collective-permute-start(bf16[256,512]{1,0:T(8,128)(2,1)} %get-tuple-element.35), channel_id=1, source_target_pairs={{0,2},{2,4},{4,6},{6,0},{1,3},{3,5},{5,7},{7,1},{8,10},{10,12},{12... | collective-permute-start | bytes 786440 | tf_op jit(solution)/shard_map/ppermute | solution.py:185
  15.7 2.4 %collective-permute-start.1 = (bf16[256,512]{1,0:T(8,128)(2,1)}, bf16[256,512]{1,0:T(8,128)(2,1)S(1)}, u32[]{:S(2)}, u32[]{:S(2)}) collective-permute-start(bf16[256,512]{1,0:T(8,128)(2,1)} %get-tuple-element.36), channel_id=1, source_target_pairs={{0,4},{2,6},{4,0},{6,2},{1,5},{3,7},{5,1},{7,3},{8,12},{10,14},{12... | collective-permute-start | bytes 786440 | tf_op jit(solution)/shard_map/ppermute | solution.py:185
  18.1 1.2 %collective-permute-start.2 = (bf16[256,512]{1,0:T(8,128)(2,1)}, bf16[256,512]{1,0:T(8,128)(2,1)S(1)}, u32[]{:S(2)}, u32[]{:S(2)}) collective-permute-start(bf16[256,512]{1,0:T(8,128)(2,1)} %get-tuple-element.37), channel_id=1, source_target_pairs={{0,6},{2,0},{4,2},{6,4},{1,7},{3,1},{5,3},{7,5},{8,14},{10,8},{12,... | collective-permute-start | bytes 786440 | tf_op jit(solution)/shard_map/ppermute | solution.py:185
  19.3 4.8 %all-to-all-done.kv_ref.refs_4_ = bf16[8,256,256]{2,1,0:T(8,128)(2,1)S(1)} async-done(((bf16[8,256,256]{2,1,0:T(8,128)(2,1)}), bf16[8,256,256]{2,1,0:T(8,128)(2,1)S(1)}, u32[]{:S(2)}, u32[]{:S(2)}) %all-to-all-start) | async-done | bytes 1048608 | tf_op jit(solution)/shard_map/all_to_all | solution.py:217
  24.1 0.6 swap_send.1
  24.7 0.6 collective-permute-start.3
  25.3 0.1 fusion
  25.3 0.2 reduce_window_sum.11
  25.5 0.2 select_reduce_fusion
  25.7 2.1 %slots.1 = bf16[256,32,128]{2,1,0:T(8,128)(2,1)} custom-call(s32[128]{0:T(128)S(1)} %multiply_add_fusion.target_ref, bf16[8,256,256]{2,1,0:T(8,128)(2,1)S(1)} %all-to-all-done.kv_ref.refs_4_), custom_call_target="tpu_custom_call" | custom-call | bytes 3145728 | tf_op jit(solution)/shard_map/slots/pallas_call | solution.py:30
  27.9 14.1 %all-to-all-start.1 = ((bf16[256,32,128]{2,1,0:T(8,128)(2,1)}), bf16[256,32,128]{2,1,0:T(8,128)(2,1)}, u32[]{:S(2)}, u32[]{:S(2)}) async-start(bf16[256,32,128]{2,1,0:T(8,128)(2,1)} %slots.1), calls=%async_computation.1 | async-start | bytes 4194304 | tf_op jit(solution)/shard_map/all_to_all | solution.py:242
  42.0 0.0 collective-permute-done.3.refs_4_
  42.0 0.4 collective-permute-start.7
  42.3 0.0 collective-permute-start.8
  42.3 0.0 collective-permute-done.refs_1_
  42.3 2.7 %collective-permute-start.9 = (bf16[256,768]{1,0:T(8,128)(2,1)}, bf16[256,768]{1,0:T(8,128)(2,1)}, u32[]{:S(2)}, u32[]{:S(2)}) collective-permute-start(bf16[256,768]{1,0:T(8,128)(2,1)} %get-tuple-element.51), channel_id=1, source_target_pairs={{0,6},{2,0},{4,2},{6,4},{1,7},{3,1},{5,3},{7,5},{8,14},{10,8},{12,... | collective-permute-start | bytes 1179656 | tf_op jit(solution)/shard_map/ppermute | solution.py:185
  45.0 0.0 collective-permute-done.1.refs_2_
  45.0 0.0 collective-permute-done.2.refs_3_
  45.0 0.0 copy-done.4
  45.0 9.9 %attend.2 = (bf16[256,512]{1,0:T(8,128)(2,1)S(1)}, bf16[256,512]{1,0:T(8,128)(2,1)S(1)}, bf16[256,512]{1,0:T(8,128)(2,1)S(1)}, bf16[256,512]{1,0:T(8,128)(2,1)S(1)}) custom-call(s32[2]{0:T(128)S(1)} %pad_add_fusion.where_ref, bf16[256,512]{1,0:T(8,128)(2,1)S(1)} %copy-done.4, bf16[256,512]{1,0:T(8,128)(2,1)S(1)} %collective-permute-done.refs_1_, ...), custom_call_target="tpu_custom_call" | custom-call | flops 199999995904 | bytes 4194304 | tf_op jit(solution)/shard_map/attend/pallas_call | solution.py:30
  55.0 1.6 %collective-permute-start.4 = (bf16[256,512]{1,0:T(8,128)(2,1)S(1)}, bf16[256,512]{1,0:T(8,128)(2,1)S(1)}, u32[]{:S(2)}, u32[]{:S(2)}) collective-permute-start(bf16[256,512]{1,0:T(8,128)(2,1)S(1)} %get-tuple-element.45), channel_id=1, source_target_pairs={{0,4},{2,6},{4,0},{6,2},{1,5},{3,7},{5,1},{7,3},{8,12},{10,14},{12... | collective-permute-start | bytes 786440 | tf_op jit(solution)/shard_map/ppermute | solution.py:185
  56.5 0.0 collective-permute-start.5
  56.5 0.0 collective-permute-done.7.refs_1_
  56.5 2.7 %collective-permute-start.6 = (bf16[256,512]{1,0:T(8,128)(2,1)S(1)}, bf16[256,512]{1,0:T(8,128)(2,1)S(1)}, u32[]{:S(2)}, u32[]{:S(2)}) collective-permute-start(bf16[256,512]{1,0:T(8,128)(2,1)S(1)} %get-tuple-element.47), channel_id=1, source_target_pairs={{0,6},{2,0},{4,2},{6,4},{1,7},{3,1},{5,3},{7,5},{8,14},{10,8},{12,... | collective-permute-start | bytes 786440 | tf_op jit(solution)/shard_map/ppermute | solution.py:185
  59.2 4.6 %collective-permute-done.8.refs_2_ = bf16[256,768]{1,0:T(8,128)(2,1)} collective-permute-done((bf16[256,768]{1,0:T(8,128)(2,1)}, bf16[256,768]{1,0:T(8,128)(2,1)}, u32[]{:S(2)}, u32[]{:S(2)}) %collective-permute-start.8) | collective-permute-done | bytes 393248 | tf_op jit(solution)/shard_map/ppermute | solution.py:185
  63.8 0.0 collective-permute-done.9.refs_3_
  63.8 10.1 %attend.3 = (bf16[256,512]{1,0:T(8,128)(2,1)S(1)}, bf16[256,512]{1,0:T(8,128)(2,1)S(1)}, bf16[256,512]{1,0:T(8,128)(2,1)S(1)}, bf16[256,512]{1,0:T(8,128)(2,1)S(1)}) custom-call(s32[2]{0:T(128)S(1)} %pad_add_fusion.where_ref, bf16[256,768]{1,0:T(8,128)(2,1)S(1)} %get-tuple-element.48.refs_0_, bf16[256,768]{1,0:T(8,128)(2,1)} %collective-permute-done.7.refs_1_, ...), custom_call_target="tpu_custom_call" | custom-call | flops 10000000000 | bytes 4194304 | tf_op jit(solution)/shard_map/attend/pallas_call | solution.py:30
  73.9 0.4 collective-permute-start.10
  74.4 0.0 collective-permute-start.11
  74.4 0.0 collective-permute-done.4.refs_1_
  74.4 2.7 %collective-permute-start.12 = (bf16[256,512]{1,0:T(8,128)(2,1)S(1)}, bf16[256,512]{1,0:T(8,128)(2,1)S(1)}, u32[]{:S(2)}, u32[]{:S(2)}) collective-permute-start(bf16[256,512]{1,0:T(8,128)(2,1)S(1)} %get-tuple-element.56), channel_id=1, source_target_pairs={{0,6},{2,0},{4,2},{6,4},{1,7},{3,1},{5,3},{7,5},{8,14},{10,8},{12,... | collective-permute-start | bytes 786440 | tf_op jit(solution)/shard_map/ppermute | solution.py:185
  77.1 0.0 collective-permute-done.5.refs_2_
  77.1 0.0 collective-permute-done.6.refs_3_
  77.1 5.6 %collective-permute-done.10.refs_5_ = bf16[256,512]{1,0:T(8,128)(2,1)S(1)} collective-permute-done((bf16[256,512]{1,0:T(8,128)(2,1)S(1)}, bf16[256,512]{1,0:T(8,128)(2,1)S(1)}, u32[]{:S(2)}, u32[]{:S(2)}) %collective-permute-start.10) | collective-permute-done | bytes 262176 | tf_op jit(solution)/shard_map/ppermute | solution.py:185
  82.7 6.8 %collective-permute-done.11.refs_6_ = bf16[256,512]{1,0:T(8,128)(2,1)S(1)} collective-permute-done((bf16[256,512]{1,0:T(8,128)(2,1)S(1)}, bf16[256,512]{1,0:T(8,128)(2,1)S(1)}, u32[]{:S(2)}, u32[]{:S(2)}) %collective-permute-start.11) | collective-permute-done | bytes 262176 | tf_op jit(solution)/shard_map/ppermute | solution.py:185
  89.5 0.0 collective-permute-done.12.refs_7_
  89.5 2.0 %gather_out.1 = bf16[256,4096]{1,0:T(8,128)(2,1)} custom-call(s32[2]{0:T(128)S(1)} %pad_add_fusion.where_ref, bf16[256,512]{1,0:T(8,128)(2,1)S(1)} %get-tuple-element.44.refs_0_, bf16[256,512]{1,0:T(8,128)(2,1)S(1)} %collective-permute-done.4.refs_1_, bf16[256,512]{1,0:T(8,128)(2,1)S(1)} %collective-permute-done.5.refs_2_, ...), custom_call_target="tpu_custom_call" | custom-call | bytes 4194304 | tf_op jit(solution)/shard_map/gather_out/pallas_call | solution.py:30
  91.5 1.9 %all-to-all-done.1.a_ref = bf16[256,32,128]{2,1,0:T(8,128)(2,1)} async-done(((bf16[256,32,128]{2,1,0:T(8,128)(2,1)}), bf16[256,32,128]{2,1,0:T(8,128)(2,1)}, u32[]{:S(2)}, u32[]{:S(2)}) %all-to-all-start.1) | async-done | bytes 2097184 | tf_op jit(solution)/shard_map/all_to_all | solution.py:242
  93.4 2.4 %caches.1 = (bf16[256,16,128]{2,1,0:T(8,128)(2,1)}, bf16[256,16,128]{2,1,0:T(8,128)(2,1)}) custom-call(bf16[256,32,128]{2,1,0:T(8,128)(2,1)} %all-to-all-done.1.a_ref), custom_call_target="tpu_custom_call" | custom-call | bytes 4194304 | tf_op jit(solution)/shard_map/caches/pallas_call | solution.py:30
  (7 shorter events, 0.0 us)
Async XLA Ops:
  0.6 8.8 %copy-start = (bf16[1,256,4096]{2,1,0:T(8,128)(2,1)S(1)}, bf16[1,256,4096]{2,1,0:T(8,128)(2,1)}, u32[]{:S(2)}) copy-start(bf16[1,256,4096]{2,1,0:T(8,128)(2,1)} %param.4) | copy-start | bytes 6291460
  2.9 21.2 %all-to-all-start = ((bf16[8,256,256]{2,1,0:T(8,128)(2,1)}), bf16[8,256,256]{2,1,0:T(8,128)(2,1)S(1)}, u32[]{:S(2)}, u32[]{:S(2)}) async-start(bf16[8,256,256]{2,1,0:T(8,128)(2,1)} %kv_send.1), calls=%async_computation | async-start | bytes 2097152 | tf_op jit(solution)/shard_map/all_to_all | solution.py:217
  9.4 1.0 %copy-start.1 = (bf16[1,256,1024]{2,1,0:T(8,128)(2,1)S(1)}, bf16[1,256,1024]{2,1,0:T(8,128)(2,1)}, u32[]{:S(2)}) copy-start(bf16[1,256,1024]{2,1,0:T(8,128)(2,1)} %param.5) | copy-start | bytes 1572868
  10.4 1.0 %copy-start.2 = (bf16[1,256,1024]{2,1,0:T(8,128)(2,1)S(1)}, bf16[1,256,1024]{2,1,0:T(8,128)(2,1)}, u32[]{:S(2)}) copy-start(bf16[1,256,1024]{2,1,0:T(8,128)(2,1)} %param.6) | copy-start | bytes 1572868
  11.5 13.8 %copy-start.5 = (s32[1,128,1]{1,2,0:T(1,128)S(1)}, s32[1,128,1]{1,2,0:T(1,128)}, u32[]{:S(2)}) copy-start(s32[1,128,1]{1,2,0:T(1,128)} %param.7) | copy-start | bytes 1540
  13.5 0.7 copy-start.3
  14.2 28.1 %collective-permute-start = (bf16[256,512]{1,0:T(8,128)(2,1)}, bf16[256,512]{1,0:T(8,128)(2,1)S(1)}, u32[]{:S(2)}, u32[]{:S(2)}) collective-permute-start(bf16[256,512]{1,0:T(8,128)(2,1)} %get-tuple-element.35), channel_id=1, source_target_pairs={{0,2},{2,4},{4,6},{6,0},{1,3},{3,5},{5,7},{7,1},{8,10},{10,12},{12... | collective-permute-start | bytes 786440 | tf_op jit(solution)/shard_map/ppermute | solution.py:185
  15.7 29.3 %collective-permute-start.1 = (bf16[256,512]{1,0:T(8,128)(2,1)}, bf16[256,512]{1,0:T(8,128)(2,1)S(1)}, u32[]{:S(2)}, u32[]{:S(2)}) collective-permute-start(bf16[256,512]{1,0:T(8,128)(2,1)} %get-tuple-element.36), channel_id=1, source_target_pairs={{0,4},{2,6},{4,0},{6,2},{1,5},{3,7},{5,1},{7,3},{8,12},{10,14},{12... | collective-permute-start | bytes 786440 | tf_op jit(solution)/shard_map/ppermute | solution.py:185
  18.1 26.9 %collective-permute-start.2 = (bf16[256,512]{1,0:T(8,128)(2,1)}, bf16[256,512]{1,0:T(8,128)(2,1)S(1)}, u32[]{:S(2)}, u32[]{:S(2)}) collective-permute-start(bf16[256,512]{1,0:T(8,128)(2,1)} %get-tuple-element.37), channel_id=1, source_target_pairs={{0,6},{2,0},{4,2},{6,4},{1,7},{3,1},{5,3},{7,5},{8,14},{10,8},{12,... | collective-permute-start | bytes 786440 | tf_op jit(solution)/shard_map/ppermute | solution.py:185
  24.7 17.3 %collective-permute-start.3 = (bf16[4,256,256]{2,1,0:T(8,128)(2,1)S(1)}, bf16[4,256,256]{2,1,0:T(8,128)(2,1)S(1)}, u32[]{:S(2)}, u32[]{:S(2)}) collective-permute-start(bf16[4,256,256]{2,1,0:T(8,128)(2,1)S(1)} %swap_send.1), channel_id=1, source_target_pairs={{0,1},{1,0},{2,3},{3,2},{4,5},{5,4},{6,7},{7,6},{8,9},{9,8},{10,11... | collective-permute-start | bytes 1572872 | tf_op jit(solution)/shard_map/ppermute | solution.py:180
  27.8 17.2 %copy-start.4 = (bf16[256,512]{1,0:T(8,128)(2,1)S(1)}, bf16[256,512]{1,0:T(8,128)(2,1)}, u32[]{:S(2)}) copy-start(bf16[256,512]{1,0:T(8,128)(2,1)} %copy-done.3) | copy-start | bytes 786436
  27.9 65.5 %all-to-all-start.1 = ((bf16[256,32,128]{2,1,0:T(8,128)(2,1)}), bf16[256,32,128]{2,1,0:T(8,128)(2,1)}, u32[]{:S(2)}, u32[]{:S(2)}) async-start(bf16[256,32,128]{2,1,0:T(8,128)(2,1)} %slots.1), calls=%async_computation.1 | async-start | bytes 4194304 | tf_op jit(solution)/shard_map/all_to_all | solution.py:242
  42.0 14.6 %collective-permute-start.7 = (bf16[256,768]{1,0:T(8,128)(2,1)}, bf16[256,768]{1,0:T(8,128)(2,1)}, u32[]{:S(2)}, u32[]{:S(2)}) collective-permute-start(bf16[256,768]{1,0:T(8,128)(2,1)} %get-tuple-element.49), channel_id=1, source_target_pairs={{0,4},{2,6},{4,0},{6,2},{1,5},{3,7},{5,1},{7,3},{8,12},{10,14},{12... | collective-permute-start | bytes 1179656 | tf_op jit(solution)/shard_map/ppermute | solution.py:185
  42.3 21.5 %collective-permute-start.8 = (bf16[256,768]{1,0:T(8,128)(2,1)}, bf16[256,768]{1,0:T(8,128)(2,1)}, u32[]{:S(2)}, u32[]{:S(2)}) collective-permute-start(bf16[256,768]{1,0:T(8,128)(2,1)} %get-tuple-element.50), channel_id=1, source_target_pairs={{0,2},{2,4},{4,6},{6,0},{1,3},{3,5},{5,7},{7,1},{8,10},{10,12},{12... | collective-permute-start | bytes 1179656 | tf_op jit(solution)/shard_map/ppermute | solution.py:185
  42.3 21.5 %collective-permute-start.9 = (bf16[256,768]{1,0:T(8,128)(2,1)}, bf16[256,768]{1,0:T(8,128)(2,1)}, u32[]{:S(2)}, u32[]{:S(2)}) collective-permute-start(bf16[256,768]{1,0:T(8,128)(2,1)} %get-tuple-element.51), channel_id=1, source_target_pairs={{0,6},{2,0},{4,2},{6,4},{1,7},{3,1},{5,3},{7,5},{8,14},{10,8},{12,... | collective-permute-start | bytes 1179656 | tf_op jit(solution)/shard_map/ppermute | solution.py:185
  55.0 19.4 %collective-permute-start.4 = (bf16[256,512]{1,0:T(8,128)(2,1)S(1)}, bf16[256,512]{1,0:T(8,128)(2,1)S(1)}, u32[]{:S(2)}, u32[]{:S(2)}) collective-permute-start(bf16[256,512]{1,0:T(8,128)(2,1)S(1)} %get-tuple-element.45), channel_id=1, source_target_pairs={{0,4},{2,6},{4,0},{6,2},{1,5},{3,7},{5,1},{7,3},{8,12},{10,14},{12... | collective-permute-start | bytes 786440 | tf_op jit(solution)/shard_map/ppermute | solution.py:185
  56.5 20.5 %collective-permute-start.5 = (bf16[256,512]{1,0:T(8,128)(2,1)S(1)}, bf16[256,512]{1,0:T(8,128)(2,1)S(1)}, u32[]{:S(2)}, u32[]{:S(2)}) collective-permute-start(bf16[256,512]{1,0:T(8,128)(2,1)S(1)} %get-tuple-element.46), channel_id=1, source_target_pairs={{0,2},{2,4},{4,6},{6,0},{1,3},{3,5},{5,7},{7,1},{8,10},{10,12},{12... | collective-permute-start | bytes 786440 | tf_op jit(solution)/shard_map/ppermute | solution.py:185
  56.5 20.5 %collective-permute-start.6 = (bf16[256,512]{1,0:T(8,128)(2,1)S(1)}, bf16[256,512]{1,0:T(8,128)(2,1)S(1)}, u32[]{:S(2)}, u32[]{:S(2)}) collective-permute-start(bf16[256,512]{1,0:T(8,128)(2,1)S(1)} %get-tuple-element.47), channel_id=1, source_target_pairs={{0,6},{2,0},{4,2},{6,4},{1,7},{3,1},{5,3},{7,5},{8,14},{10,8},{12,... | collective-permute-start | bytes 786440 | tf_op jit(solution)/shard_map/ppermute | solution.py:185
  73.9 8.7 %collective-permute-start.10 = (bf16[256,512]{1,0:T(8,128)(2,1)S(1)}, bf16[256,512]{1,0:T(8,128)(2,1)S(1)}, u32[]{:S(2)}, u32[]{:S(2)}) collective-permute-start(bf16[256,512]{1,0:T(8,128)(2,1)S(1)} %get-tuple-element.54), channel_id=1, source_target_pairs={{0,4},{2,6},{4,0},{6,2},{1,5},{3,7},{5,1},{7,3},{8,12},{10,14},{12... | collective-permute-start | bytes 786440 | tf_op jit(solution)/shard_map/ppermute | solution.py:185
  74.4 15.1 %collective-permute-start.11 = (bf16[256,512]{1,0:T(8,128)(2,1)S(1)}, bf16[256,512]{1,0:T(8,128)(2,1)S(1)}, u32[]{:S(2)}, u32[]{:S(2)}) collective-permute-start(bf16[256,512]{1,0:T(8,128)(2,1)S(1)} %get-tuple-element.55), channel_id=1, source_target_pairs={{0,2},{2,4},{4,6},{6,0},{1,3},{3,5},{5,7},{7,1},{8,10},{10,12},{12... | collective-permute-start | bytes 786440 | tf_op jit(solution)/shard_map/ppermute | solution.py:185
  74.4 15.1 %collective-permute-start.12 = (bf16[256,512]{1,0:T(8,128)(2,1)S(1)}, bf16[256,512]{1,0:T(8,128)(2,1)S(1)}, u32[]{:S(2)}, u32[]{:S(2)}) collective-permute-start(bf16[256,512]{1,0:T(8,128)(2,1)S(1)} %get-tuple-element.56), channel_id=1, source_target_pairs={{0,6},{2,0},{4,2},{6,4},{1,7},{3,1},{5,3},{7,5},{8,14},{10,8},{12,... | collective-permute-start | bytes 786440 | tf_op jit(solution)/shard_map/ppermute | solution.py:185
